TPU v7x, 256 devices: a whole 4x4x8 slice. The times are simulated.
256 devices in a mesh: blk: 128 (over z, x_lo, y, core), seg: 2 (over x_hi).
Axes of the slice: x: 4 (x_hi: 2, x_lo: 2; x = x_hi * 2 + x_lo), y: 4, z: 8, core: 2. Of those that a mesh axis runs over, the one named last changes fastest.
Arguments:
- recording: bfloat16 [2, 5120, 16384], P('seg', 'blk'), may hold values from -6 to 6
- filter_taps: float32 [31], replicated, may hold values from -1 to 1
- pair_offsets: int32 [128, 2], P('blk'), may hold values from 0 to 3, all different within a row
Outputs:
- correlations: bfloat16 [128, 2, 128, 200, 128], P('blk', None, None, 'seg')
Inputs may be any that keep to these rules, and one draw needn't show every extreme that they name: `pair_offsets`: each row holds 2 different offsets, and every offset below 4 appears in some row.
All inputs are finite; a program needn't handle non-finite values.
Results may differ from a plain program's by a relative error of at most 0.0056.
Values may be sent and summed in bfloat16 or wider, within the bound.
No kernel may reach another device: no remote copies, remote signals or barrier semaphores. Data moves between devices by JAX's collectives and lax.ppermute only.
A program may use at most 192 MiB of HBM per device.

v0:
```python
import math

import jax
import jax.numpy as jnp
from jax import lax
from jax.sharding import PartitionSpec as P

DECIM = 5
FILT = 31
MAXLAG = 100
BAND = 4
SLOTS = 2


def from_behind(shard, axis, by):
    peers = lax.axis_size(axis)
    return lax.ppermute(shard, axis, [(i, (i + by) % peers) for i in range(peers)])


def condition(segment, filter_taps):
    length = segment.shape[0]
    sample_count = length // DECIM
    groups = -(-FILT // DECIM)
    half_taps = FILT // 2
    zero_padded_length = DECIM * (sample_count + groups)
    padded = jnp.pad(
        segment.astype(jnp.float32), ((half_taps, zero_padded_length - half_taps - length), (0, 0))
    )
    stacked = padded.reshape(sample_count + groups, DECIM, segment.shape[1])
    weights = jnp.pad(filter_taps, (0, DECIM * groups - FILT)).reshape(groups, DECIM)
    filtered = jnp.zeros((sample_count, segment.shape[1]), jnp.float32)
    for group_index in range(groups):
        filtered = filtered + jnp.einsum(
            "mpc,p->mc",
            stacked[group_index : group_index + sample_count],
            weights[group_index],
            precision=lax.Precision.HIGHEST,
        )
    return filtered


def normalize(filtered):
    spread = jnp.sqrt(jnp.mean(filtered * filtered, axis=0) + 1e-06)
    return (filtered / spread).astype(jnp.bfloat16)


def lag_products(left_channel_block, right_block, first_lag, lag_count):
    length = left_channel_block.shape[1]
    padded = jnp.pad(right_block, ((0, 0), (MAXLAG, MAXLAG), (0, 0)))
    window = lax.dynamic_slice_in_dim(padded, first_lag, length + lag_count - 1, 1)
    per_lag = []
    for lag_offset in range(lag_count):
        per_lag.append(
            jnp.einsum(
                "vum,vuq->mq",
                left_channel_block,
                window[:, lag_offset : lag_offset + length],
                preferred_element_type=jnp.float32,
            )
        )
    return jnp.stack(per_lag, axis=1)


def on_device(recording, filter_taps, pair_offsets):
    arrived = lax.all_to_all(recording, "blk", split_axis=2, concat_axis=1, tiled=True)
    own_series = normalize(condition(arrived[0], filter_taps))
    segment_count = lax.axis_size("seg")
    total_time = segment_count * own_series.shape[0]
    total_lag_count = 2 * MAXLAG
    series = lax.all_gather(own_series[None], "seg", axis=0, tiled=True)
    fetched = [series]
    current = series
    for hop_count in range(1, BAND):
        current = from_behind(current, "blk", -1)
        fetched.append(current)
    fetched_all = jnp.stack(fetched)
    offsets = pair_offsets[0]
    lag_share = total_lag_count // segment_count
    first_lag = lax.axis_index("seg") * lag_share
    per_slot = [
        lag_products(
            series,
            lax.dynamic_index_in_dim(fetched_all, offsets[slot_index], 0, keepdims=False),
            first_lag,
            lag_share,
        )
        for slot_index in range(SLOTS)
    ]
    result = jnp.stack(per_slot)[None] / math.sqrt(total_time)
    return result.astype(jnp.bfloat16)


def solution(mesh):
    placed = (P("seg", "blk", None), P(), P("blk", None))
    return jax.shard_map(
        on_device,
        mesh=mesh,
        in_specs=placed,
        out_specs=P("blk", None, None, "seg", None),
        check_vma=False,
    )
```

profile of v0, /device:TPU:27, one launch (start us, length us, event | category | flops | bytes accessed | tf_op | source)
XLA Modules:
  0.0 493.9 jit_solution(11943638192794853429)
XLA Ops:
  0.0 16.3 %copy.407 = bf16[1,40,16384]{1,0,2:T(2,128)(2,1)} copy(bf16[1,40,16384]{2,1,0:T(8,128)(2,1)} %param.3) | data formatting | bytes 2621440 | tf_op args[0]
  16.8 90.8 %reduce = bf16[16384,40]{1,0:T(8,128)(2,1)} reduce(bf16[16384,1,40]{2,1,0:T(2,128)(2,1)} %bitcast.1268, bf16[]{:T(256)} %broadcast.26), dimensions={1}, to_apply=%bitcast.1058.reduce_sub_computation | reduce | bytes 2621442
  107.6 9.0 %reshape.294 = bf16[128,2,2560]{2,1,0:T(2,128)(2,1)S(1)} reshape(bf16[16384,40]{1,0:T(8,128)(2,1)} %reduce) | data formatting | bytes 2621440
  116.6 47.7 %all_to_all.4 = bf16[128,2,2560]{2,1,0:T(2,128)(2,1)S(1)} all-to-all(bf16[128,2,2560]{2,1,0:T(2,128)(2,1)S(1)} %reshape.294), channel_id=1, replica_groups=mesh['blk'=128,'seg'=2] {'blk'}, dimensions={0} | all-to-all | bytes 2621440 | tf_op jit(solution)/shard_map/all_to_all | solution.py:65
  164.4 17.6 %reshape.295 = bf16[16384,1,40]{2,1,0:T(2,128)(2,1)} reshape(bf16[128,2,2560]{2,1,0:T(2,128)(2,1)S(1)} %all_to_all.4) | data formatting | bytes 2621440
  182.0 15.2 %copy.408 = bf16[1,40,16384]{2,1,0:T(8,128)(2,1)S(1)} copy(bf16[1,40,16384]{1,0,2:T(2,128)(2,1)} %bitcast.1269) | data formatting | bytes 2621440 | tf_op jit(solution)/shard_map/all_to_all | solution.py:65
  199.1 3.7 pad_slice_fusion.3
  202.7 3.7 slice.684.clone
  206.4 2.6 fusion.607
  209.1 4.2 fusion.611
  213.3 2.4 slice.681.clone
  215.7 2.6 fusion.613
  218.9 2.6 fusion.609
  221.5 2.7 slice.691.clone
  224.2 2.7 fusion.605
  226.8 2.4 slice.694.clone
  229.3 2.6 fusion.603
  232.4 1.9 fusion.601
  234.3 2.1 multiply_reduce_fusion
  236.4 9.9 %all-gather = bf16[2048,128]{1,0:T(8,128)(2,1)S(1)} all-gather(bf16[1024,128]{1,0:T(8,128)(2,1)S(1)} %divide_convert_fusion), channel_id=2, replica_groups=mesh['blk'=128,'seg'=2] {'seg'}, dimensions={0}, use_global_device_ids=true | all-gather | bytes 786432 | tf_op jit(solution)/shard_map/all_gather | solution.py:70
  247.3 10.6 %collective-permute-done = bf16[2,1024,128]{2,1,0:T(8,128)(2,1)S(1)} collective-permute-done((bf16[2,1024,128]{2,1,0:T(8,128)(2,1)S(1)}, bf16[2,1024,128]{2,1,0:T(8,128)(2,1)S(1)}, u32[]{:S(2)}, u32[]{:S(2)}) %collective-permute-start) | collective-permute-done | bytes 524320 | tf_op jit(solution)/shard_map/ppermute | solution.py:17
  257.9 11.6 %collective-permute-done.1 = bf16[2,1024,128]{2,1,0:T(8,128)(2,1)S(1)} collective-permute-done((bf16[2,1024,128]{2,1,0:T(8,128)(2,1)S(1)}, bf16[2,1024,128]{2,1,0:T(8,128)(2,1)S(1)}, u32[]{:S(2)}, u32[]{:S(2)}) %collective-permute-start.1) | collective-permute-done | bytes 524320 | tf_op jit(solution)/shard_map/ppermute | solution.py:17
  273.9 7.4 %collective-permute-done.2 = bf16[2,1024,128]{2,1,0:T(8,128)(2,1)S(1)} collective-permute-done((bf16[2,1024,128]{2,1,0:T(8,128)(2,1)S(1)}, bf16[2,1024,128]{2,1,0:T(8,128)(2,1)S(1)}, u32[]{:S(2)}, u32[]{:S(2)}) %collective-permute-start.2) | collective-permute-done | bytes 524320 | tf_op jit(solution)/shard_map/ppermute | solution.py:17
  484.3 9.4 %fusion = bf16[1,2,128,100,128]{4,2,3,1,0:T(8,128)(2,1)} fusion(f32[1,1,128,100,128]{4,2,3,1,0:T(8,128)} %bitcast.433, f32[1,1,128,100,128]{4,2,3,1,0:T(8,128)} %bitcast.230), kind=kLoop, calls=%fused_computation.1 | loop fusion | flops 9830400 | bytes 19660800 | tf_op jit(solution)/shard_map/convert_element_type | solution.py:90
  (223 shorter events, 208.2 us)
Async XLA Ops:
  199.0 7.4 %copy-start.2 = (f32[31]{0:T(128)S(1)}, f32[31]{0:T(128)}, u32[]{:S(2)}) copy-start(f32[31]{0:T(128)} %param.4) | copy-start | bytes 376
  202.7 15.6 %copy-start.1 = (bf16[5120,128]{1,0:T(8,128)(2,1)S(1)}, bf16[5120,128]{1,0:T(8,128)(2,1)}, u32[]{:S(2)}) copy-start(bf16[5120,128]{1,0:T(8,128)(2,1)} %get-tuple-element.11) | copy-start | bytes 3932164
  221.5 10.4 %copy-start = (bf16[5120,128]{1,0:T(8,128)(2,1)S(1)}, bf16[5120,128]{1,0:T(8,128)(2,1)}, u32[]{:S(2)}) copy-start(bf16[5120,128]{1,0:T(8,128)(2,1)} %get-tuple-element.14) | copy-start | bytes 3932164
  231.9 37.8 %copy-start.3 = (s32[1,2]{1,0:T(1,128)S(1)}, s32[1,2]{1,0:T(1,128)}, u32[]{:S(2)}) copy-start(s32[1,2]{1,0:T(1,128)} %param.5) | copy-start | bytes 28
  246.3 11.6 %collective-permute-start = (bf16[2,1024,128]{2,1,0:T(8,128)(2,1)S(1)}, bf16[2,1024,128]{2,1,0:T(8,128)(2,1)S(1)}, u32[]{:S(2)}, u32[]{:S(2)}) collective-permute-start(bf16[2,1024,128]{2,1,0:T(8,128)(2,1)S(1)} %bitcast.1280), channel_id=1, source_target_pairs={{0,254},{2,0},{4,2},{6,4},{8,6},{10,8},{12,10},{14,12},{16,14},{18... | collective-permute-start | bytes 1572872 | tf_op jit(solution)/shard_map/ppermute | solution.py:17
  257.9 11.6 %collective-permute-start.1 = (bf16[2,1024,128]{2,1,0:T(8,128)(2,1)S(1)}, bf16[2,1024,128]{2,1,0:T(8,128)(2,1)S(1)}, u32[]{:S(2)}, u32[]{:S(2)}) collective-permute-start(bf16[2,1024,128]{2,1,0:T(8,128)(2,1)S(1)} %collective-permute-done), channel_id=1, source_target_pairs={{0,254},{2,0},{4,2},{6,4},{8,6},{10,8},{12,10},{14,12},{16,14},{18... | collective-permute-start | bytes 1572872 | tf_op jit(solution)/shard_map/ppermute | solution.py:17
  269.5 11.8 %collective-permute-start.2 = (bf16[2,1024,128]{2,1,0:T(8,128)(2,1)S(1)}, bf16[2,1024,128]{2,1,0:T(8,128)(2,1)S(1)}, u32[]{:S(2)}, u32[]{:S(2)}) collective-permute-start(bf16[2,1024,128]{2,1,0:T(8,128)(2,1)S(1)} %collective-permute-done.1), channel_id=1, source_target_pairs={{0,254},{2,0},{4,2},{6,4},{8,6},{10,8},{12,10},{14,12},{16,14},{18... | collective-permute-start | bytes 1572872 | tf_op jit(solution)/shard_map/ppermute | solution.py:17
where the time goes:
time: 503 us; the launch traced here: 494 us
  matrix products  222 us (44%)
  other arithmetic  103 us (20%)
  local copies, waits for them, and re-layouts  77.1 us (15%)
  blocking collectives  57.6 us (11%)
  waiting for transfers between devices  29.6 us (6%)
    dot_general x200, matrix products, lag_products(): jnp.einsum('vum,vuq->mq', left_channel_block, window[:, lag_offset:lag_of...  203 us
    unnamed x1, other arithmetic  90.8 us
    all_to_all x1, blocking collectives, on_device(): lax.all_to_all(recording, 'blk', split_axis=2, concat_axis=1, tiled=True)  47.7 us
    unnamed x13, local copies, waits for them, and re-layouts  43.8 us
    ppermute x3, waiting for transfers between devices, from_behind(): lax.ppermute(shard, axis, [(i, (i + by) % peers) for i in range(peers)])  29.6 us
    dot_general x7, matrix products, condition(): jnp.einsum('mpc,p->mc', stacked[group_index:group_index + sample_count],...  19.3 us
    slice x7, local copies, waits for them, and re-layouts, condition(): stacked[group_index:group_index + sample_count]  15.9 us
    all_to_all x1, local copies, waits for them, and re-layouts, on_device(): lax.all_to_all(recording, 'blk', split_axis=2, concat_axis=1, tiled=True)  15.2 us
  transfers between devices with their start and end apart: 3, of which 3 were waited for; matrix products, arithmetic and copies ran while one was open for 0% of the time, Pallas kernels for 0%

commit v1 on v0

v1 whole, which is shorter than its diff:
```python
import math

import jax
import jax.numpy as jnp
from jax import lax
from jax.experimental import pallas as pl
from jax.experimental.pallas import tpu as pltpu
from jax.sharding import PartitionSpec as P

DECIM = 5
FILT = 31
MAXLAG = 100
BAND = 4
SLOTS = 2
CB = 128
BLOCKS = 128
TS = 1024
RAW = 40
ROWS = 8
EDGE = 16
SHIFTS = 10
PAIR = 2
STEPS = MAXLAG // (SHIFTS * PAIR)
PAD = TS + 128
REACH = MAXLAG - SHIFTS
WIDE = -(-(TS + REACH) // 8) * 8
CHUNK = 256
VMEM = pl.BlockSpec(memory_space=pltpu.VMEM)
SMEM = pl.BlockSpec(memory_space=pltpu.SMEM)
F32 = jnp.float32
BF16 = jnp.bfloat16


def split3(x):
    parts = []
    for _ in range(3):
        part = x.astype(BF16)
        parts.append(part)
        x = x - part.astype(F32)
    return jnp.concatenate(parts, 0)


def fold3(total):
    return (total[:ROWS] + total[ROWS : 2 * ROWS]) + total[2 * ROWS :]


def inner_kernel(band_ref, own_ref, out_ref):
    band = split3(band_ref[:, EDGE : EDGE + RAW])
    for i in range(BLOCKS * CB // CHUNK):
        at = slice(i * CHUNK, (i + 1) * CHUNK)
        out_ref[:, at] = fold3(jnp.dot(band, own_ref[:, at], preferred_element_type=F32))


def inner_filter(band, own):
    return pl.pallas_call(
        inner_kernel,
        in_specs=[VMEM] * 2,
        out_specs=VMEM,
        out_shape=jax.ShapeDtypeStruct((ROWS, BLOCKS * CB), F32),
        compiler_params=pltpu.CompilerParams(vmem_limit_bytes=24 << 20),
        name="inner_filter",
    )(band, own)


def edge_kernel(band_ref, inner_ref, left_ref, right_ref, out_ref):
    left_band = split3(band_ref[:, :EDGE])
    right_band = split3(band_ref[:, EDGE + RAW :])
    for i in range(BLOCKS * CB // CHUNK):
        at = slice(i * CHUNK, (i + 1) * CHUNK)
        edges = jnp.dot(left_band, left_ref[:, at], preferred_element_type=F32)
        edges += jnp.dot(right_band, right_ref[:, at], preferred_element_type=F32)
        rows = (inner_ref[:, at] + fold3(edges)).astype(BF16)
        for j in range(CHUNK // CB):
            for ahead in range(BAND):
                owner = (i * (CHUNK // CB) + j - ahead) % BLOCKS
                out_ref[owner, ahead] = rows[:, j * CB : (j + 1) * CB]


def edge_filter(band, inner, left, right):
    return pl.pallas_call(
        edge_kernel,
        in_specs=[VMEM] * 4,
        out_specs=VMEM,
        out_shape=jax.ShapeDtypeStruct((BLOCKS, BAND, ROWS, CB), BF16),
        compiler_params=pltpu.CompilerParams(vmem_limit_bytes=24 << 20),
        name="edge_filter",
    )(band, inner, left, right)


def pick_kernel(offsets_ref, all_ref, first_ref, second_ref):
    first_ref[0] = all_ref[:, 0]
    first_ref[1] = all_ref[:, offsets_ref[0, 0]]
    second_ref[0] = all_ref[:, offsets_ref[0, 1]]


def pick(offsets, arrived):
    return pl.pallas_call(
        pick_kernel,
        in_specs=[SMEM, VMEM],
        out_specs=[VMEM, VMEM],
        out_shape=[jax.ShapeDtypeStruct((n, BLOCKS, ROWS, CB), BF16) for n in (2, 1)],
        compiler_params=pltpu.CompilerParams(vmem_limit_bytes=24 << 20),
        name="pick",
    )(offsets, arrived)


def wide_rows(x):
    return x.reshape(TS, CB).astype(F32)


def inverse_spread(x):
    return 1.0 / jnp.sqrt(jnp.sum(x * x, axis=0, keepdims=True) / TS + 1e-6)


def build_left(ahead, x, lhs, column, lpad):
    column[...] = jnp.broadcast_to(inverse_spread(x), (CB, CB)).T * (1.0 / math.sqrt(2 * TS))
    lpad[:, 0:TS] = x.T
    lpad[:, TS:PAD] = jnp.zeros((CB, PAD - TS), F32)
    lpad[...] = pltpu.roll(lpad[...], jnp.where(ahead, 0, PAD - SHIFTS), 1)
    for g in range(SHIFTS):
        moved = lpad[...] if g == 0 else pltpu.roll(lpad[...], g, 1)
        lhs[g * CB : (g + 1) * CB, :] = moved[:, :TS].astype(BF16)


def build_right(ahead, x, win, fac, column, wide):
    fac[...] = column[...] * inverse_spread(x)

    def place(off):
        if off:
            wide[0:off, :] = jnp.zeros((off, CB), F32)
        if off + TS < WIDE:
            wide[off + TS : WIDE, :] = jnp.zeros((WIDE - off - TS, CB), F32)
        wide[off : off + TS, :] = x

    pl.when(ahead)(lambda: place(0))
    pl.when(jnp.logical_not(ahead))(lambda: place(REACH))
    for h in range(STEPS * PAIR):
        at = SHIFTS * h
        k = h % PAIR
        win[h // PAIR, :, k * CB : (k + 1) * CB] = wide[at : at + TS, :].astype(BF16)


def emit(acc, fac, out_ref, add_ref=None):
    for g in range(SHIFTS):
        for k in range(PAIR):
            value = acc[g * CB : (g + 1) * CB, k * CB : (k + 1) * CB] * fac
            if add_ref is not None:
                value += add_ref[0, k * SHIFTS + g]
            out_ref[0, k * SHIFTS + g] = value.astype(out_ref.dtype)


def own_kernel(seg_ref, offsets_ref, all_ref, out_ref, lhs, win, fac, column, wide, lpad, acc):
    step = pl.program_id(0)
    ahead = seg_ref[0] == 1

    @pl.when(step == 0)
    def _():
        build_left(ahead, wide_rows(all_ref[:, 0]), lhs, column, lpad)
        for q in range(SLOTS):
            x = wide_rows(all_ref[:, offsets_ref[0, q]])
            build_right(ahead, x, win.at[pl.ds(q * STEPS, STEPS)], fac.at[q], column, wide)

    acc[...] = jnp.dot(lhs[...], win[step], preferred_element_type=F32)
    emit(acc, fac[step // STEPS], out_ref)


def cost(products):
    return pl.CostEstimate(flops=2 * products * CB * CB * TS, bytes_accessed=8 << 20, transcendentals=0)


def own_products(seg, offsets, arrived):
    return pl.pallas_call(
        own_kernel,
        grid_spec=pltpu.PrefetchScalarGridSpec(
            num_scalar_prefetch=2,
            grid=(SLOTS * STEPS,),
            in_specs=[pl.BlockSpec((BLOCKS, BAND, ROWS, CB), lambda h, s, o: (0, 0, 0, 0))],
            out_specs=pl.BlockSpec((1, PAIR * SHIFTS, CB, CB), lambda h, s, o: (h // STEPS, h % STEPS, 0, 0)),
            scratch_shapes=[
                pltpu.VMEM((SHIFTS * CB, TS), BF16),
                pltpu.VMEM((SLOTS * STEPS, TS, PAIR * CB), BF16),
                pltpu.VMEM((SLOTS, CB, CB), F32),
                pltpu.VMEM((CB, CB), F32),
                pltpu.VMEM((WIDE, CB), F32),
                pltpu.VMEM((CB, PAD), F32),
                pltpu.VMEM((SHIFTS * CB, PAIR * CB), F32),
            ],
        ),
        out_shape=jax.ShapeDtypeStruct((SLOTS, MAXLAG, CB, CB), F32),
        compiler_params=pltpu.CompilerParams(vmem_limit_bytes=32 << 20, dimension_semantics=("arbitrary",)),
        cost_estimate=cost(SLOTS * MAXLAG),
        name="own_products",
    )(seg, offsets, arrived)


def first_kernel(seg_ref, other_ref, own_ref, out_ref, lhs, column, win, fac, wide, lpad, acc):
    step = pl.program_id(0)
    ahead = seg_ref[0] == 1

    @pl.when(step == 0)
    def _():
        build_left(ahead, wide_rows(other_ref[0]), lhs, column, lpad)
        build_right(ahead, wide_rows(other_ref[1]), win, fac, column, wide)

    acc[...] = jnp.dot(lhs[...], win[step], preferred_element_type=F32)
    emit(acc, fac[...], out_ref, own_ref)


def second_kernel(seg_ref, other_ref, lhs, column, own_ref, _, out_ref, win, fac, wide, acc):
    step = pl.program_id(0)

    @pl.when(step == 0)
    def _():
        build_right(seg_ref[0] == 1, wide_rows(other_ref[0]), win, fac, column, wide)

    acc[...] = jnp.dot(lhs[...], win[step], preferred_element_type=F32)
    emit(acc, fac[...], out_ref, own_ref)


def slot_spec(q):
    return pl.BlockSpec((1, PAIR * SHIFTS, CB, CB), lambda h, s: (q, h, 0, 0))


def fixed(*shape):
    return pl.BlockSpec(shape, lambda h, s: (0,) * len(shape))


def first_products(seg, other, own):
    return pl.pallas_call(
        first_kernel,
        grid_spec=pltpu.PrefetchScalarGridSpec(
            num_scalar_prefetch=1,
            grid=(STEPS,),
            in_specs=[fixed(2, BLOCKS, ROWS, CB), slot_spec(0)],
            out_specs=[slot_spec(0), fixed(SHIFTS * CB, TS), fixed(CB, CB)],
            scratch_shapes=[
                pltpu.VMEM((STEPS, TS, PAIR * CB), BF16),
                pltpu.VMEM((CB, CB), F32),
                pltpu.VMEM((WIDE, CB), F32),
                pltpu.VMEM((CB, PAD), F32),
                pltpu.VMEM((SHIFTS * CB, PAIR * CB), F32),
            ],
        ),
        out_shape=[
            jax.ShapeDtypeStruct((SLOTS, MAXLAG, CB, CB), BF16),
            jax.ShapeDtypeStruct((SHIFTS * CB, TS), BF16),
            jax.ShapeDtypeStruct((CB, CB), F32),
        ],
        compiler_params=pltpu.CompilerParams(vmem_limit_bytes=32 << 20, dimension_semantics=("arbitrary",)),
        cost_estimate=cost(MAXLAG),
        name="first_products",
    )(seg, other, own)


def second_products(seg, other, lhs, column, own, lags):
    return pl.pallas_call(
        second_kernel,
        grid_spec=pltpu.PrefetchScalarGridSpec(
            num_scalar_prefetch=1,
            grid=(STEPS,),
            in_specs=[
                fixed(1, BLOCKS, ROWS, CB),
                fixed(SHIFTS * CB, TS),
                fixed(CB, CB),
                slot_spec(1),
                pl.BlockSpec(memory_space=pl.ANY),
            ],
            out_specs=slot_spec(1),
            scratch_shapes=[
                pltpu.VMEM((STEPS, TS, PAIR * CB), BF16),
                pltpu.VMEM((CB, CB), F32),
                pltpu.VMEM((WIDE, CB), F32),
                pltpu.VMEM((SHIFTS * CB, PAIR * CB), F32),
            ],
        ),
        out_shape=jax.ShapeDtypeStruct((SLOTS, MAXLAG, CB, CB), BF16),
        input_output_aliases={5: 0},
        compiler_params=pltpu.CompilerParams(vmem_limit_bytes=32 << 20, dimension_semantics=("arbitrary",)),
        cost_estimate=cost(MAXLAG),
        name="second_products",
    )(seg, other, lhs, column, own, lags)


def banded(filter_taps):
    width = 2 * EDGE + RAW
    rows = [jnp.pad(filter_taps, (1 + DECIM * m, width - 1 - DECIM * m - FILT)) for m in range(ROWS)]
    return jnp.stack(rows)


def on_device(recording, filter_taps, pair_offsets):
    raw = recording[0]
    last = BLOCKS - 1
    left = lax.ppermute(raw[RAW - EDGE :], "blk", [(i, i + 1) for i in range(last)])
    right = lax.ppermute(raw[:EDGE], "blk", [(i + 1, i) for i in range(last)])
    band = banded(filter_taps)
    dealt = edge_filter(band, inner_filter(band, raw), left, right)
    arrived = lax.all_to_all(dealt, "blk", split_axis=0, concat_axis=0, tiled=True)
    seg = lax.axis_index("seg").astype(jnp.int32).reshape(1)
    swap = [(0, 1), (1, 0)]
    first, second = pick(pair_offsets, arrived)
    first = lax.ppermute(first, "seg", swap)
    second = lax.ppermute(second, "seg", swap)
    own = own_products(seg, pair_offsets, arrived)
    lags, lhs, column = first_products(seg, first, own)
    lags = second_products(seg, second, lhs, column, own, lags)
    return jnp.swapaxes(lags, 1, 2)[None]


def solution(mesh):
    placed = (P("seg", "blk", None), P(), P("blk", None))
    return jax.shard_map(
        on_device,
        mesh=mesh,
        in_specs=placed,
        out_specs=P("blk", None, None, "seg", None),
        check_vma=False,
    )
```

time: 503 us -> 97.6 us (0.19)
  the two profiles are of different devices: /device:TPU:27 before, /device:TPU:2 now
where the time goes in v1:
time: 97.6 us; the launch traced here: 97.4 us
  waiting for transfers between devices  43.9 us (45%)
  Pallas kernels  26.9 us (28%)
  starting transfers between devices  22.8 us (23%)
  local copies, waits for them, and re-layouts  3.65 us (4%)
    all_to_all x1, waiting for transfers between devices, on_device(): lax.all_to_all(dealt, 'blk', split_axis=0, concat_axis=0, tiled=True)  29.5 us
    all_to_all x1, starting transfers between devices, on_device(): lax.all_to_all(dealt, 'blk', split_axis=0, concat_axis=0, tiled=True)  13 us
    pallas_call x1, Pallas kernels, own_products(): pl.pallas_call(own_kernel, grid_spec=pltpu.PrefetchScalarGridSpec(num_sca...  11.3 us
    pallas_call x1, Pallas kernels, first_products(): pl.pallas_call(first_kernel, grid_spec=pltpu.PrefetchScalarGridSpec(num_s...  6.85 us
    ppermute x1, waiting for transfers between devices, on_device(): first = lax.ppermute(first, 'seg', swap)  6.62 us
    ppermute x1, waiting for transfers between devices, on_device(): lax.ppermute(raw[RAW - EDGE:], 'blk', [(i, i + 1) for i in range(last)])  5.93 us
    pallas_call x1, Pallas kernels, second_products(): pl.pallas_call(second_kernel, grid_spec=pltpu.PrefetchScalarGridSpec(num_...  5.83 us
    ppermute x1, starting transfers between devices, on_device(): right = lax.ppermute(raw[:EDGE], 'blk', [(i + 1, i) for i in range(last)])  4.33 us
  transfers between devices with their start and end apart: 5, of which 4 were waited for; matrix products, arithmetic and copies ran while one was open for 1% of the time, Pallas kernels for 19%

profile of v1, /device:TPU:2, one launch (start us, length us, event | category | flops | bytes accessed | tf_op | source)
XLA Modules:
  0.0 97.4 jit_solution(14784836959955223239)
XLA Ops:
  0.0 0.0 copy-start.1
  0.0 1.3 %slice_bitcast_fusion = (bf16[16,16384]{1,0:T(8,128)(2,1)S(1)}, bf16[16,16384]{1,0:T(8,128)(2,1)S(1)}) fusion(bf16[1,40,16384]{2,1,0:T(8,128)(2,1)} %param.3), kind=kLoop, calls=%fused_computation | loop fusion | bytes 2097152 | tf_op jit(solution)/shard_map/slice | solution.py:294
  1.3 4.3 %collective-permute-start.1 = (bf16[16,16384]{1,0:T(8,128)(2,1)S(1)}, bf16[16,16384]{1,0:T(8,128)(2,1)S(1)}, u32[]{:S(2)}, u32[]{:S(2)}) collective-permute-start(bf16[16,16384]{1,0:T(8,128)(2,1)S(1)} %get-tuple-element.15), channel_id=1, source_target_pairs={{2,0},{4,2},{6,4},{8,6},{10,8},{12,10},{14,12},{16,14},{18,16},{20... | collective-permute-start | bytes 1572872 | tf_op jit(solution)/shard_map/ppermute | solution.py:294
  5.6 1.9 %collective-permute-start = (bf16[16,16384]{1,0:T(8,128)(2,1)S(1)}, bf16[16,16384]{1,0:T(8,128)(2,1)S(1)}, u32[]{:S(2)}, u32[]{:S(2)}) collective-permute-start(bf16[16,16384]{1,0:T(8,128)(2,1)S(1)} %get-tuple-element.16), channel_id=1, source_target_pairs={{0,2},{2,4},{4,6},{6,8},{8,10},{10,12},{12,14},{14,16},{16,18},{18... | collective-permute-start | bytes 1572872 | tf_op jit(solution)/shard_map/ppermute | solution.py:293
  7.6 1.0 %pad_bitcast_fusion = (f32[1,72]{1,0:T(1,128)S(1)}, f32[1,72]{1,0:T(1,128)S(1)}, f32[1,72]{1,0:T(1,128)S(1)}, f32[1,72]{1,0:T(1,128)S(1)}, f32[1,72]{1,0:T(1,128...) fusion(f32[31]{0:T(128)} %param.4), kind=kLoop, calls=%fused_computation.2 | loop fusion | bytes 2428 | tf_op jit(solution)/shard_map/stack | solution.py:287
  8.6 0.0 copy-start
  8.6 1.3 %copy-done = bf16[1,40,16384]{2,1,0:T(8,128)(2,1)S(1)} copy-done((bf16[1,40,16384]{2,1,0:T(8,128)(2,1)S(1)}, bf16[1,40,16384]{2,1,0:T(8,128)(2,1)}, u32[]{:S(2)}) %copy-start) | copy-done | bytes 1310744
  9.9 0.5 inner_filter.1.inner_ref
  10.4 1.9 %collective-permute-done.1.right_ref = bf16[16,16384]{1,0:T(8,128)(2,1)S(1)} collective-permute-done((bf16[16,16384]{1,0:T(8,128)(2,1)S(1)}, bf16[16,16384]{1,0:T(8,128)(2,1)S(1)}, u32[]{:S(2)}, u32[]{:S(2)}) %collective-permute-start.1) | collective-permute-done | bytes 524320 | tf_op jit(solution)/shard_map/ppermute | solution.py:294
  12.3 5.9 %collective-permute-done.left_ref = bf16[16,16384]{1,0:T(8,128)(2,1)S(1)} collective-permute-done((bf16[16,16384]{1,0:T(8,128)(2,1)S(1)}, bf16[16,16384]{1,0:T(8,128)(2,1)S(1)}, u32[]{:S(2)}, u32[]{:S(2)}) %collective-permute-start) | collective-permute-done | bytes 524320 | tf_op jit(solution)/shard_map/ppermute | solution.py:293
  18.2 1.7 %edge_filter.1 = bf16[128,4,8,128]{3,2,1,0:T(8,128)(2,1)} custom-call(f32[8,72]{1,0:T(8,128)S(1)} %stack.35.band_ref, f32[8,16384]{1,0:T(8,128)S(1)} %inner_filter.1.inner_ref, bf16[16,16384]{1,0:T(8,128)(2,1)S(1)} %collective-permute-done.left_ref, bf16[16,16384]{1,0:T(8,128)(2,1)S(1)} %collective-permute-done.1.right_ref), custom_call_target="tpu_custom_call" | custom-call | tf_op jit(solution)/shard_map/edge_filter/pallas_call | solution.py:80
  20.0 13.0 %all-to-all-start = ((bf16[128,4,8,128]{3,2,1,0:T(8,128)(2,1)}), bf16[128,4,8,128]{3,2,1,0:T(8,128)(2,1)S(1)}, u32[]{:S(2)}, u32[]{:S(2)}) async-start(bf16[128,4,8,128]{3,2,1,0:T(8,128)(2,1)} %edge_filter.1), calls=%async_computation | async-start | bytes 2097152 | tf_op jit(solution)/shard_map/all_to_all | solution.py:297
  32.9 29.5 %all-to-all-done.all_ref = bf16[128,4,8,128]{3,2,1,0:T(8,128)(2,1)S(1)} async-done(((bf16[128,4,8,128]{3,2,1,0:T(8,128)(2,1)}), bf16[128,4,8,128]{3,2,1,0:T(8,128)(2,1)S(1)}, u32[]{:S(2)}, u32[]{:S(2)}) %all-to-all-start) | async-done | bytes 1048608 | tf_op jit(solution)/shard_map/all_to_all | solution.py:297
  62.4 0.0 copy-done.1
  62.4 0.7 pick.1
  63.1 2.2 %collective-permute-start.2 = (bf16[1,128,8,128]{3,2,1,0:T(8,128)(2,1)S(1)}, bf16[1,128,8,128]{3,2,1,0:T(8,128)(2,1)S(1)}, u32[]{:S(2)}, u32[]{:S(2)}) collective-permute-start(bf16[1,128,8,128]{3,2,1,0:T(8,128)(2,1)S(1)} %get-tuple-element.10), channel_id=1, source_target_pairs={{0,1},{1,0},{2,3},{3,2},{4,5},{5,4},{6,7},{7,6},{8,9},{9,8},{10,11... | collective-permute-start | bytes 786440 | tf_op jit(solution)/shard_map/ppermute | solution.py:302
  65.3 1.4 %collective-permute-start.3 = (bf16[2,128,8,128]{3,2,1,0:T(8,128)(2,1)S(1)}, bf16[2,128,8,128]{3,2,1,0:T(8,128)(2,1)S(1)}, u32[]{:S(2)}, u32[]{:S(2)}) collective-permute-start(bf16[2,128,8,128]{3,2,1,0:T(8,128)(2,1)S(1)} %get-tuple-element.11), channel_id=1, source_target_pairs={{0,1},{1,0},{2,3},{3,2},{4,5},{5,4},{6,7},{7,6},{8,9},{9,8},{10,11... | collective-permute-start | bytes 1572872 | tf_op jit(solution)/shard_map/ppermute | solution.py:301
  66.7 11.3 %own_products.1.own_ref = f32[2,100,128,128]{3,2,1,0:T(8,128)S(1)} custom-call(s32[1]{0:T(128)} %bitcast.seg_ref, s32[1,2]{1,0:T(1,128)S(1)} %copy-done.1, bf16[128,4,8,128]{3,2,1,0:T(8,128)(2,1)S(1)} %all-to-all-done.all_ref), custom_call_target="tpu_custom_call" | custom-call | flops 6710886400 | bytes 8388608 | tf_op jit(solution)/shard_map/own_products/pallas_call | solution.py:172
  78.1 6.6 %collective-permute-done.3.other_ref = bf16[2,128,8,128]{3,2,1,0:T(8,128)(2,1)S(1)} collective-permute-done((bf16[2,128,8,128]{3,2,1,0:T(8,128)(2,1)S(1)}, bf16[2,128,8,128]{3,2,1,0:T(8,128)(2,1)S(1)}, u32[]{:S(2)}, u32[]{:S(2)}) %collective-permute-start.3) | collective-permute-done | bytes 524320 | tf_op jit(solution)/shard_map/ppermute | solution.py:301
  84.7 6.9 %first_products.1 = (bf16[2,100,128,128]{3,2,1,0:T(8,128)(2,1)}, bf16[1280,1024]{1,0:T(8,128)(2,1)S(1)}, f32[128,128]{1,0:T(8,128)S(1)}) custom-call(s32[1]{0:T(128)} %bitcast.seg_ref, bf16[2,128,8,128]{3,2,1,0:T(8,128)(2,1)S(1)} %collective-permute-done.3.other_ref, f32[2,100,128,128]{3,2,1,0:T(8,128)S(1)} %own_products.1.own_ref), custom_call_target="tpu_custom_call" | custom-call | flops 3355443200 | bytes 8388608 | tf_op jit(solution)/shard_map/first_products/pallas_call | solution.py:229
  91.5 0.0 collective-permute-done.2.other_ref
  91.5 5.8 %second_products.1 = bf16[2,100,128,128]{3,2,1,0:T(8,128)(2,1)} custom-call(s32[1]{0:T(128)} %bitcast.seg_ref, bf16[1,128,8,128]{3,2,1,0:T(8,128)(2,1)S(1)} %collective-permute-done.2.other_ref, bf16[1280,1024]{1,0:T(8,128)(2,1)S(1)} %get-tuple-element.12.lhs, f32[128,128]{1,0:T(8,128)S(1)} %get-tuple-element.13.column, ...), custom_call_target="tpu_custom_call", output_to_operand_aliasing={{}: (5, {})} | custom-call | flops 3355443200 | bytes 8388608 | tf_op jit(solution)/shard_map/second_products/pallas_call | solution.py:256
  (1 shorter events, 0.0 us)
Async XLA Ops:
  0.0 62.4 %copy-start.1 = (s32[1,2]{1,0:T(1,128)S(1)}, s32[1,2]{1,0:T(1,128)}, u32[]{:S(2)}) copy-start(s32[1,2]{1,0:T(1,128)} %offsets_ref.3) | copy-start | bytes 28
  1.3 11.0 %collective-permute-start.1 = (bf16[16,16384]{1,0:T(8,128)(2,1)S(1)}, bf16[16,16384]{1,0:T(8,128)(2,1)S(1)}, u32[]{:S(2)}, u32[]{:S(2)}) collective-permute-start(bf16[16,16384]{1,0:T(8,128)(2,1)S(1)} %get-tuple-element.15), channel_id=1, source_target_pairs={{2,0},{4,2},{6,4},{8,6},{10,8},{12,10},{14,12},{16,14},{18,16},{20... | collective-permute-start | bytes 1572872 | tf_op jit(solution)/shard_map/ppermute | solution.py:294
  5.6 12.6 %collective-permute-start = (bf16[16,16384]{1,0:T(8,128)(2,1)S(1)}, bf16[16,16384]{1,0:T(8,128)(2,1)S(1)}, u32[]{:S(2)}, u32[]{:S(2)}) collective-permute-start(bf16[16,16384]{1,0:T(8,128)(2,1)S(1)} %get-tuple-element.16), channel_id=1, source_target_pairs={{0,2},{2,4},{4,6},{6,8},{8,10},{10,12},{12,14},{14,16},{16,18},{18... | collective-permute-start | bytes 1572872 | tf_op jit(solution)/shard_map/ppermute | solution.py:293
  8.6 1.3 %copy-start = (bf16[1,40,16384]{2,1,0:T(8,128)(2,1)S(1)}, bf16[1,40,16384]{2,1,0:T(8,128)(2,1)}, u32[]{:S(2)}) copy-start(bf16[1,40,16384]{2,1,0:T(8,128)(2,1)} %param.3) | copy-start | bytes 3932164
  20.0 42.4 %all-to-all-start = ((bf16[128,4,8,128]{3,2,1,0:T(8,128)(2,1)}), bf16[128,4,8,128]{3,2,1,0:T(8,128)(2,1)S(1)}, u32[]{:S(2)}, u32[]{:S(2)}) async-start(bf16[128,4,8,128]{3,2,1,0:T(8,128)(2,1)} %edge_filter.1), calls=%async_computation | async-start | bytes 2097152 | tf_op jit(solution)/shard_map/all_to_all | solution.py:297
  63.1 28.4 %collective-permute-start.2 = (bf16[1,128,8,128]{3,2,1,0:T(8,128)(2,1)S(1)}, bf16[1,128,8,128]{3,2,1,0:T(8,128)(2,1)S(1)}, u32[]{:S(2)}, u32[]{:S(2)}) collective-permute-start(bf16[1,128,8,128]{3,2,1,0:T(8,128)(2,1)S(1)} %get-tuple-element.10), channel_id=1, source_target_pairs={{0,1},{1,0},{2,3},{3,2},{4,5},{5,4},{6,7},{7,6},{8,9},{9,8},{10,11... | collective-permute-start | bytes 786440 | tf_op jit(solution)/shard_map/ppermute | solution.py:302
  65.3 19.4 %collective-permute-start.3 = (bf16[2,128,8,128]{3,2,1,0:T(8,128)(2,1)S(1)}, bf16[2,128,8,128]{3,2,1,0:T(8,128)(2,1)S(1)}, u32[]{:S(2)}, u32[]{:S(2)}) collective-permute-start(bf16[2,128,8,128]{3,2,1,0:T(8,128)(2,1)S(1)} %get-tuple-element.11), channel_id=1, source_target_pairs={{0,1},{1,0},{2,3},{3,2},{4,5},{5,4},{6,7},{7,6},{8,9},{9,8},{10,11... | collective-permute-start | bytes 1572872 | tf_op jit(solution)/shard_map/ppermute | solution.py:301

commit v2 on v1

v2 whole, which is shorter than its diff:
```python
import functools
import math

import jax
import jax.numpy as jnp
from jax import lax
from jax.experimental import pallas as pl
from jax.experimental.pallas import tpu as pltpu
from jax.sharding import PartitionSpec as P

DECIM = 5
FILT = 31
MAXLAG = 100
DEALT = (0, 2)
SLOTS = 2
CB = 128
BLOCKS = 128
TS = 1024
RAW = 40
ROWS = 8
EDGE = 16
SHIFTS = 10
PAIR = 2
STEPS = MAXLAG // (SHIFTS * PAIR)
PAD = TS + 128
REACH = MAXLAG - SHIFTS
WIDE = -(-(TS + REACH) // 8) * 8
CHUNK = 256
VMEM = pl.BlockSpec(memory_space=pltpu.VMEM)
SMEM = pl.BlockSpec(memory_space=pltpu.SMEM)
F32 = jnp.float32
BF16 = jnp.bfloat16


def split3(x):
    parts = []
    for _ in range(3):
        part = x.astype(BF16)
        parts.append(part)
        x = x - part.astype(F32)
    return jnp.concatenate(parts, 0)


def fold3(total):
    return (total[:ROWS] + total[ROWS : 2 * ROWS]) + total[2 * ROWS :]


def inner_kernel(band_ref, own_ref, out_ref):
    band = split3(band_ref[:, EDGE : EDGE + RAW])
    for i in range(BLOCKS * CB // CHUNK):
        at = slice(i * CHUNK, (i + 1) * CHUNK)
        out_ref[:, at] = fold3(jnp.dot(band, own_ref[:, at], preferred_element_type=F32))


def inner_filter(band, own):
    return pl.pallas_call(
        inner_kernel,
        in_specs=[VMEM] * 2,
        out_specs=VMEM,
        out_shape=jax.ShapeDtypeStruct((ROWS, BLOCKS * CB), F32),
        compiler_params=pltpu.CompilerParams(vmem_limit_bytes=24 << 20),
        name="inner_filter",
    )(band, own)


def edge_kernel(band_ref, inner_ref, left_ref, right_ref, out_ref):
    left_band = split3(band_ref[:, :EDGE])
    right_band = split3(band_ref[:, EDGE + RAW :])
    for i in range(BLOCKS * CB // CHUNK):
        at = slice(i * CHUNK, (i + 1) * CHUNK)
        edges = jnp.dot(left_band, left_ref[:, at], preferred_element_type=F32)
        edges += jnp.dot(right_band, right_ref[:, at], preferred_element_type=F32)
        rows = (inner_ref[:, at] + fold3(edges)).astype(BF16)
        for j in range(CHUNK // CB):
            for place, ahead in enumerate(DEALT):
                owner = (i * (CHUNK // CB) + j - ahead) % BLOCKS
                out_ref[owner, place] = rows[:, j * CB : (j + 1) * CB]


def edge_filter(band, inner, left, right):
    return pl.pallas_call(
        edge_kernel,
        in_specs=[VMEM] * 4,
        out_specs=VMEM,
        out_shape=jax.ShapeDtypeStruct((BLOCKS, len(DEALT), ROWS, CB), BF16),
        compiler_params=pltpu.CompilerParams(vmem_limit_bytes=24 << 20),
        name="edge_filter",
    )(band, inner, left, right)


BLOCK = jax.ShapeDtypeStruct((BLOCKS, ROWS, CB), BF16)


def part_kernel(odd_ref, arrived_ref, zero_ref, two_ref, pair_ref):
    zero_ref[...] = arrived_ref[:, 0]
    two_ref[...] = arrived_ref[:, 1]
    pair_ref[...] = arrived_ref[:, 1 - odd_ref[0]]


def part(odd, arrived):
    return pl.pallas_call(
        part_kernel,
        in_specs=[SMEM, VMEM],
        out_specs=[VMEM] * 3,
        out_shape=[BLOCK] * 3,
        compiler_params=pltpu.CompilerParams(vmem_limit_bytes=24 << 20),
        name="part",
    )(odd, arrived)


def pick_kernel(q, offsets_ref, *refs):
    for ahead in range(4):

        @pl.when(offsets_ref[0, q] == ahead)
        def _(ahead=ahead):
            refs[-1][...] = refs[ahead][...]


def pick(q, offsets, blocks):
    return pl.pallas_call(
        functools.partial(pick_kernel, q),
        in_specs=[SMEM] + [VMEM] * len(blocks),
        out_specs=VMEM,
        out_shape=BLOCK,
        compiler_params=pltpu.CompilerParams(vmem_limit_bytes=24 << 20),
        name="pick",
    )(offsets, *blocks)


def wide_rows(x):
    return x.reshape(TS, CB).astype(F32)


def inverse_spread(x):
    return 1.0 / jnp.sqrt(jnp.sum(x * x, axis=0, keepdims=True) / TS + 1e-6)


def pad_left(ahead, x, column, lpad):
    column[...] = jnp.broadcast_to(inverse_spread(x), (CB, CB)).T * (1.0 / math.sqrt(2 * TS))
    lpad[:, 0:TS] = x.T
    lpad[:, TS:PAD] = jnp.zeros((CB, PAD - TS), F32)
    lpad[...] = pltpu.roll(lpad[...], jnp.where(ahead, 0, PAD - SHIFTS), 1)


def left_kernel(seg_ref, own_ref, lhs, column, lpad):
    pad_left(seg_ref[0] == 1, wide_rows(own_ref[...]), column, lpad)
    for g in range(SHIFTS):
        moved = lpad[...] if g == 0 else pltpu.roll(lpad[...], g, 1)
        lhs[g * CB : (g + 1) * CB, :] = moved[:, :TS].astype(BF16)


LEFT = [jax.ShapeDtypeStruct((SHIFTS * CB, TS), BF16), jax.ShapeDtypeStruct((CB, CB), F32)]


def left_rows(seg, own):
    return pl.pallas_call(
        left_kernel,
        in_specs=[SMEM, VMEM],
        out_specs=[VMEM] * 2,
        out_shape=LEFT,
        scratch_shapes=[pltpu.VMEM((CB, PAD), F32)],
        compiler_params=pltpu.CompilerParams(vmem_limit_bytes=24 << 20),
        cost_estimate=pl.CostEstimate(flops=1 << 20, bytes_accessed=9 << 20, transcendentals=0),
        name="left_rows",
    )(seg, own)


def build_right(ahead, x, win, fac, column, wide):
    fac[...] = column[...] * inverse_spread(x)

    def place(off):
        if off:
            wide[0:off, :] = jnp.zeros((off, CB), F32)
        if off + TS < WIDE:
            wide[off + TS : WIDE, :] = jnp.zeros((WIDE - off - TS, CB), F32)
        wide[off : off + TS, :] = x

    pl.when(ahead)(lambda: place(0))
    pl.when(jnp.logical_not(ahead))(lambda: place(REACH))
    for h in range(STEPS * PAIR):
        at = SHIFTS * h
        k = h % PAIR
        win[h // PAIR, :, k * CB : (k + 1) * CB] = wide[at : at + TS, :].astype(BF16)


def own_kernel(seg_ref, lhs, column, right0_ref, right1_ref, out_ref, fac, win, wide):
    ahead = seg_ref[0] == 1
    for q, ref in enumerate((right0_ref, right1_ref)):
        build_right(ahead, wide_rows(ref[...]), win.at[pl.ds(q * STEPS, STEPS)], fac.at[q], column, wide)

    def multiply(step, carry):
        out_ref[step] = jnp.dot(lhs[...], win[step], preferred_element_type=F32)
        return carry

    lax.fori_loop(0, SLOTS * STEPS, multiply, 0, unroll=5)


def cost(products):
    return pl.CostEstimate(flops=2 * products * CB * CB * TS, bytes_accessed=8 << 20, transcendentals=0)


def slot_spec(q):
    return pl.BlockSpec((1, PAIR * SHIFTS, CB, CB), lambda h, s: (q, h, 0, 0))


def fixed(*shape):
    return pl.BlockSpec(shape, lambda h, s: (0,) * len(shape))


def own_products(seg, lhs, column, rights):
    return pl.pallas_call(
        own_kernel,
        in_specs=[SMEM] + [VMEM] * 4,
        out_specs=[VMEM] * 2,
        out_shape=[
            jax.ShapeDtypeStruct((SLOTS * STEPS, SHIFTS * CB, PAIR * CB), F32),
            jax.ShapeDtypeStruct((SLOTS, CB, CB), F32),
        ],
        scratch_shapes=[
            pltpu.VMEM((SLOTS * STEPS, TS, PAIR * CB), BF16),
            pltpu.VMEM((WIDE, CB), F32),
        ],
        compiler_params=pltpu.CompilerParams(vmem_limit_bytes=28 << 20),
        cost_estimate=cost(SLOTS * MAXLAG),
        name="own_products",
    )(seg, lhs, column, *rights)


def other_kernel(seg_ref, other_ref, lhs, column, own_ref, own_fac, *refs):
    out_ref, win, fac, wide, acc = refs[-5:]
    step = pl.program_id(0)

    @pl.when(step == 0)
    def _():
        build_right(seg_ref[0] == 1, wide_rows(other_ref[...]), win, fac, column, wide)

    acc[...] = jnp.dot(lhs[...], win[step], preferred_element_type=F32)
    for g in range(SHIFTS):
        for k in range(PAIR):
            at = slice(g * CB, (g + 1) * CB), slice(k * CB, (k + 1) * CB)
            value = acc[at] * fac[...] + own_ref[(0,) + at] * own_fac[0]
            out_ref[0, k * SHIFTS + g] = value.astype(BF16)


def other_products(q, seg, other, lhs, column, own, lags):
    return pl.pallas_call(
        other_kernel,
        grid_spec=pltpu.PrefetchScalarGridSpec(
            num_scalar_prefetch=1,
            grid=(STEPS,),
            in_specs=[
                fixed(BLOCKS, ROWS, CB),
                fixed(SHIFTS * CB, TS),
                fixed(CB, CB),
                pl.BlockSpec((1, SHIFTS * CB, PAIR * CB), lambda h, s: (q * STEPS + h, 0, 0)),
                pl.BlockSpec((1, CB, CB), lambda h, s: (q, 0, 0)),
            ]
            + [pl.BlockSpec(memory_space=pl.ANY)] * len(lags),
            out_specs=slot_spec(q),
            scratch_shapes=[
                pltpu.VMEM((STEPS, TS, PAIR * CB), BF16),
                pltpu.VMEM((CB, CB), F32),
                pltpu.VMEM((WIDE, CB), F32),
                pltpu.VMEM((SHIFTS * CB, PAIR * CB), F32),
            ],
        ),
        out_shape=jax.ShapeDtypeStruct((SLOTS, MAXLAG, CB, CB), BF16),
        input_output_aliases={6: 0} if lags else {},
        compiler_params=pltpu.CompilerParams(vmem_limit_bytes=28 << 20, dimension_semantics=("arbitrary",)),
        cost_estimate=cost(MAXLAG),
        name="other_products",
    )(seg, other, lhs, column, *own, *lags)


def banded(filter_taps):
    width = 2 * EDGE + RAW
    rows = [jnp.pad(filter_taps, (1 + DECIM * m, width - 1 - DECIM * m - FILT)) for m in range(ROWS)]
    return jnp.stack(rows)


def on_device(recording, filter_taps, pair_offsets):
    raw = recording[0]
    last = BLOCKS - 1
    left = lax.ppermute(raw[RAW - EDGE :], "blk", [(i, i + 1) for i in range(last)])
    right = lax.ppermute(raw[:EDGE], "blk", [(i + 1, i) for i in range(last)])
    band = banded(filter_taps)
    dealt = edge_filter(band, inner_filter(band, raw), left, right)
    arrived = lax.all_to_all(dealt, "blk", split_axis=0, concat_axis=0, tiled=True)
    seg = lax.axis_index("seg").astype(jnp.int32).reshape(1)
    odd = (lax.axis_index("blk") % 2).astype(jnp.int32).reshape(1)
    swap = [(0, 1), (1, 0)]
    zero, two, pair = part(odd, arrived)
    one = lax.ppermute(pair, "blk", [(i, i ^ 1) for i in range(BLOCKS)])
    three = lax.ppermute(two, "blk", [(i, (i - 1) % BLOCKS) for i in range(BLOCKS)])
    other_left = lax.ppermute(zero, "seg", swap)
    lhs, column = left_rows(seg, zero)
    blocks = (zero, one, two, three)
    right = pick(0, pair_offsets, blocks)
    rights = (right, pick(1, pair_offsets, (*blocks, right)))
    other_rights = [lax.ppermute(right, "seg", swap) for right in rights]
    own = own_products(seg, lhs, column, rights)
    *own, other_left = lax.optimization_barrier((*own, other_left))
    other_lhs, other_column = left_rows(seg, other_left)
    lags = []
    for q in range(SLOTS):
        lags = [other_products(q, seg, other_rights[q], other_lhs, other_column, own, lags)]
    return jnp.swapaxes(lags[0], 1, 2)[None]


def solution(mesh):
    placed = (P("seg", "blk", None), P(), P("blk", None))
    return jax.shard_map(
        on_device,
        mesh=mesh,
        in_specs=placed,
        out_specs=P("blk", None, None, "seg", None),
        check_vma=False,
    )
```

time: 97.6 us -> 86.8 us (0.89)
  the two profiles are of different devices: /device:TPU:2 before, /device:TPU:29 now
where the time goes in v2:
time: 86.8 us; the launch traced here: 86.5 us
  waiting for transfers between devices  30.6 us (35%)
  starting transfers between devices  27.7 us (32%)
  Pallas kernels  25.6 us (29%)
  local copies, waits for them, and re-layouts  2.43 us (3%)
    all_to_all x1, waiting for transfers between devices, on_device(): lax.all_to_all(dealt, 'blk', split_axis=0, concat_axis=0, tiled=True)  17.1 us
    all_to_all x1, starting transfers between devices, on_device(): lax.all_to_all(dealt, 'blk', split_axis=0, concat_axis=0, tiled=True)  15.8 us
    pallas_call x2, Pallas kernels, other_products(): pl.pallas_call(other_kernel, grid_spec=pltpu.PrefetchScalarGridSpec(num_s...  11.6 us
    ppermute x1, waiting for transfers between devices, on_device(): lax.ppermute(two, 'blk', [(i, (i - 1) % BLOCKS) for i in range(BLOCKS)])  8.9 us
    pallas_call x1, Pallas kernels, own_products(): pl.pallas_call(own_kernel, in_specs=[SMEM] + [VMEM] * 4, out_specs=[VMEM]...  8.43 us
    ppermute x1, starting transfers between devices, on_device(): lax.ppermute(raw[RAW - EDGE:], 'blk', [(i, i + 1) for i in range(last)])  5.09 us
    ppermute x1, waiting for transfers between devices, on_device(): right = lax.ppermute(raw[:EDGE], 'blk', [(i + 1, i) for i in range(last)])  3.37 us
    ppermute x2, starting transfers between devices, on_device(): other_rights = [lax.ppermute(right, 'seg', swap) for right in rights]  3.13 us
  transfers between devices with their start and end apart: 8, of which 4 were waited for; matrix products, arithmetic and copies ran while one was open for 1% of the time, Pallas kernels for 21%

profile of v2, /device:TPU:29, one launch (start us, length us, event | category | flops | bytes accessed | tf_op | source)
XLA Modules:
  0.0 86.5 jit_solution(14744497603647620903)
XLA Ops:
  0.0 1.4 %slice_bitcast_fusion = (bf16[16,16384]{1,0:T(8,128)(2,1)S(1)}, bf16[16,16384]{1,0:T(8,128)(2,1)S(1)}) fusion(bf16[1,40,16384]{2,1,0:T(8,128)(2,1)} %param.3), kind=kLoop, calls=%fused_computation | loop fusion | bytes 2097152 | tf_op jit(solution)/shard_map/slice | solution.py:285
  1.4 2.6 %collective-permute-start.1 = (bf16[16,16384]{1,0:T(8,128)(2,1)S(1)}, bf16[16,16384]{1,0:T(8,128)(2,1)S(1)}, u32[]{:S(2)}, u32[]{:S(2)}) collective-permute-start(bf16[16,16384]{1,0:T(8,128)(2,1)S(1)} %get-tuple-element.29), channel_id=1, source_target_pairs={{2,0},{4,2},{6,4},{8,6},{10,8},{12,10},{14,12},{16,14},{18,16},{20... | collective-permute-start | bytes 1572872 | tf_op jit(solution)/shard_map/ppermute | solution.py:285
  4.0 5.1 %collective-permute-start = (bf16[16,16384]{1,0:T(8,128)(2,1)S(1)}, bf16[16,16384]{1,0:T(8,128)(2,1)S(1)}, u32[]{:S(2)}, u32[]{:S(2)}) collective-permute-start(bf16[16,16384]{1,0:T(8,128)(2,1)S(1)} %get-tuple-element.30), channel_id=1, source_target_pairs={{0,2},{2,4},{4,6},{6,8},{8,10},{10,12},{12,14},{14,16},{16,18},{18... | collective-permute-start | bytes 1572872 | tf_op jit(solution)/shard_map/ppermute | solution.py:284
  9.1 1.0 %pad_bitcast_fusion = (f32[1,72]{1,0:T(1,128)S(1)}, f32[1,72]{1,0:T(1,128)S(1)}, f32[1,72]{1,0:T(1,128)S(1)}, f32[1,72]{1,0:T(1,128)S(1)}, f32[1,72]{1,0:T(1,128...) fusion(f32[31]{0:T(128)} %param.4), kind=kLoop, calls=%fused_computation.2 | loop fusion | bytes 2428 | tf_op jit(solution)/shard_map/stack | solution.py:278
  10.1 0.5 inner_filter.1.inner_ref
  10.6 3.4 %collective-permute-done.1.right_ref = bf16[16,16384]{1,0:T(8,128)(2,1)S(1)} collective-permute-done((bf16[16,16384]{1,0:T(8,128)(2,1)S(1)}, bf16[16,16384]{1,0:T(8,128)(2,1)S(1)}, u32[]{:S(2)}, u32[]{:S(2)}) %collective-permute-start.1) | collective-permute-done | bytes 524320 | tf_op jit(solution)/shard_map/ppermute | solution.py:285
  14.0 1.2 %collective-permute-done.left_ref = bf16[16,16384]{1,0:T(8,128)(2,1)S(1)} collective-permute-done((bf16[16,16384]{1,0:T(8,128)(2,1)S(1)}, bf16[16,16384]{1,0:T(8,128)(2,1)S(1)}, u32[]{:S(2)}, u32[]{:S(2)}) %collective-permute-start) | collective-permute-done | bytes 524320 | tf_op jit(solution)/shard_map/ppermute | solution.py:284
  15.2 1.6 %edge_filter.1 = bf16[128,2,8,128]{3,2,1,0:T(8,128)(2,1)} custom-call(f32[8,72]{1,0:T(8,128)S(1)} %stack.35.band_ref, f32[8,16384]{1,0:T(8,128)S(1)} %inner_filter.1.inner_ref, bf16[16,16384]{1,0:T(8,128)(2,1)S(1)} %collective-permute-done.left_ref, bf16[16,16384]{1,0:T(8,128)(2,1)S(1)} %collective-permute-done.1.right_ref), custom_call_target="tpu_custom_call" | custom-call | tf_op jit(solution)/shard_map/edge_filter/pallas_call | solution.py:81
  16.7 15.8 %all-to-all-start = ((bf16[128,2,8,128]{3,2,1,0:T(8,128)(2,1)}), bf16[128,2,8,128]{3,2,1,0:T(8,128)(2,1)S(1)}, u32[]{:S(2)}, u32[]{:S(2)}) async-start(bf16[128,2,8,128]{3,2,1,0:T(8,128)(2,1)} %edge_filter.1), calls=%async_computation | async-start | bytes 1048576 | tf_op jit(solution)/shard_map/all_to_all | solution.py:288
  32.6 17.1 %all-to-all-done.arrived_ref = bf16[128,2,8,128]{3,2,1,0:T(8,128)(2,1)S(1)} async-done(((bf16[128,2,8,128]{3,2,1,0:T(8,128)(2,1)}), bf16[128,2,8,128]{3,2,1,0:T(8,128)(2,1)S(1)}, u32[]{:S(2)}, u32[]{:S(2)}) %all-to-all-start) | async-done | bytes 524320 | tf_op jit(solution)/shard_map/all_to_all | solution.py:288
  49.7 0.1 part.1
  49.8 0.5 collective-permute-start.2
  50.3 0.1 collective-permute-start.3
  50.4 0.5 collective-permute-start.5
  50.9 1.1 %left_rows.2 = (bf16[1280,1024]{1,0:T(8,128)(2,1)S(1)}, f32[128,128]{1,0:T(8,128)S(1)}) custom-call(s32[1]{0:T(128)} %bitcast.seg_ref, bf16[128,8,128]{2,1,0:T(8,128)(2,1)S(1)} %get-tuple-element.17.refs_0_.own_ref), custom_call_target="tpu_custom_call" | custom-call | flops 1048576 | bytes 9437184 | tf_op jit(solution)/shard_map/left_rows/pallas_call | solution.py:156
  52.1 8.9 %collective-permute-done.3.refs_3_ = bf16[128,8,128]{2,1,0:T(8,128)(2,1)S(1)} collective-permute-done((bf16[128,8,128]{2,1,0:T(8,128)(2,1)S(1)}, bf16[128,8,128]{2,1,0:T(8,128)(2,1)S(1)}, u32[]{:S(2)}, u32[]{:S(2)}) %collective-permute-start.3) | collective-permute-done | bytes 262176 | tf_op jit(solution)/shard_map/ppermute | solution.py:294
  61.0 0.6 pick.2.refs_4_.right0_ref
  61.6 0.1 collective-permute-start.6
  61.7 0.6 pick.3.right1_ref
  62.3 3.0 %collective-permute-start.4 = (bf16[128,8,128]{2,1,0:T(8,128)(2,1)S(1)}, bf16[128,8,128]{2,1,0:T(8,128)(2,1)S(1)}, u32[]{:S(2)}, u32[]{:S(2)}) collective-permute-start(bf16[128,8,128]{2,1,0:T(8,128)(2,1)S(1)} %pick.3.right1_ref), channel_id=1, source_target_pairs={{0,1},{1,0},{2,3},{3,2},{4,5},{5,4},{6,7},{7,6},{8,9},{9,8},{10,11... | collective-permute-start | bytes 786440 | tf_op jit(solution)/shard_map/ppermute | solution.py:300
  65.3 8.4 %own_products.1 = (f32[10,1280,256]{2,1,0:T(8,128)S(1)}, f32[2,128,128]{2,1,0:T(8,128)S(1)}) custom-call(s32[1]{0:T(128)} %bitcast.seg_ref, bf16[1280,1024]{1,0:T(8,128)(2,1)S(1)} %get-tuple-element.20.lhs, f32[128,128]{1,0:T(8,128)S(1)} %get-tuple-element.21.column, bf16[128,8,128]{2,1,0:T(8,128)(2,1)S(1)} %pick.2.refs_4_.right0_ref, ...), custom_call_target="tpu_custom_call" | custom-call | flops 6710886400 | bytes 8388608 | tf_op jit(solution)/shard_map/own_products/pallas_call | solution.py:211
  73.8 1.2 %left_rows.3 = (bf16[1280,1024]{1,0:T(8,128)(2,1)S(1)}, f32[128,128]{1,0:T(8,128)S(1)}) custom-call(s32[1]{0:T(128)} %bitcast.seg_ref, bf16[128,8,128]{2,1,0:T(8,128)(2,1)S(1)} %collective-permute-done.5.own_ref), custom_call_target="tpu_custom_call" | custom-call | flops 1048576 | bytes 9437184 | tf_op jit(solution)/shard_map/left_rows/pallas_call | solution.py:156
  75.0 5.8 %other_products.2.refs_0_ = bf16[2,100,128,128]{3,2,1,0:T(8,128)(2,1)} custom-call(s32[1]{0:T(128)} %bitcast.seg_ref, bf16[128,8,128]{2,1,0:T(8,128)(2,1)S(1)} %collective-permute-done.6.other_ref, bf16[1280,1024]{1,0:T(8,128)(2,1)S(1)} %get-tuple-element.25.lhs, f32[128,128]{1,0:T(8,128)S(1)} %get-tuple-element.26.column, ...), custom_call_target="tpu_custom_call" | custom-call | flops 3355443200 | bytes 8388608 | tf_op jit(solution)/shard_map/other_products/pallas_call | solution.py:246
  80.8 5.8 %other_products.3 = bf16[2,100,128,128]{3,2,1,0:T(8,128)(2,1)} custom-call(s32[1]{0:T(128)} %bitcast.seg_ref, bf16[128,8,128]{2,1,0:T(8,128)(2,1)S(1)} %collective-permute-done.4.other_ref, bf16[1280,1024]{1,0:T(8,128)(2,1)S(1)} %get-tuple-element.25.lhs, f32[128,128]{1,0:T(8,128)S(1)} %get-tuple-element.26.column, ...), custom_call_target="tpu_custom_call", output_to_operand_aliasing={{}: (6, {})} | custom-call | flops 3355443200 | bytes 8388608 | tf_op jit(solution)/shard_map/other_products/pallas_call | solution.py:246
  (9 shorter events, 0.0 us)
Async XLA Ops:
  0.0 10.1 %copy-start = (bf16[1,40,16384]{2,1,0:T(8,128)(2,1)S(1)}, bf16[1,40,16384]{2,1,0:T(8,128)(2,1)}, u32[]{:S(2)}) copy-start(bf16[1,40,16384]{2,1,0:T(8,128)(2,1)} %param.3) | copy-start | bytes 3932164
  1.4 12.6 %collective-permute-start.1 = (bf16[16,16384]{1,0:T(8,128)(2,1)S(1)}, bf16[16,16384]{1,0:T(8,128)(2,1)S(1)}, u32[]{:S(2)}, u32[]{:S(2)}) collective-permute-start(bf16[16,16384]{1,0:T(8,128)(2,1)S(1)} %get-tuple-element.29), channel_id=1, source_target_pairs={{2,0},{4,2},{6,4},{8,6},{10,8},{12,10},{14,12},{16,14},{18,16},{20... | collective-permute-start | bytes 1572872 | tf_op jit(solution)/shard_map/ppermute | solution.py:285
  4.0 11.2 %collective-permute-start = (bf16[16,16384]{1,0:T(8,128)(2,1)S(1)}, bf16[16,16384]{1,0:T(8,128)(2,1)S(1)}, u32[]{:S(2)}, u32[]{:S(2)}) collective-permute-start(bf16[16,16384]{1,0:T(8,128)(2,1)S(1)} %get-tuple-element.30), channel_id=1, source_target_pairs={{0,2},{2,4},{4,6},{6,8},{8,10},{10,12},{12,14},{14,16},{16,18},{18... | collective-permute-start | bytes 1572872 | tf_op jit(solution)/shard_map/ppermute | solution.py:284
  10.1 50.9 %copy-start.1 = (s32[1,2]{1,0:T(1,128)S(1)}, s32[1,2]{1,0:T(1,128)}, u32[]{:S(2)}) copy-start(s32[1,2]{1,0:T(1,128)} %offsets_ref.3) | copy-start | bytes 28
  16.7 33.0 %all-to-all-start = ((bf16[128,2,8,128]{3,2,1,0:T(8,128)(2,1)}), bf16[128,2,8,128]{3,2,1,0:T(8,128)(2,1)S(1)}, u32[]{:S(2)}, u32[]{:S(2)}) async-start(bf16[128,2,8,128]{3,2,1,0:T(8,128)(2,1)} %edge_filter.1), calls=%async_computation | async-start | bytes 1048576 | tf_op jit(solution)/shard_map/all_to_all | solution.py:288
  49.8 2.3 %collective-permute-start.2 = (bf16[128,8,128]{2,1,0:T(8,128)(2,1)S(1)}, bf16[128,8,128]{2,1,0:T(8,128)(2,1)S(1)}, u32[]{:S(2)}, u32[]{:S(2)}) collective-permute-start(bf16[128,8,128]{2,1,0:T(8,128)(2,1)S(1)} %get-tuple-element.18), channel_id=1, source_target_pairs={{0,2},{2,0},{4,6},{6,4},{8,10},{10,8},{12,14},{14,12},{16,18},{18,... | collective-permute-start | bytes 786440 | tf_op jit(solution)/shard_map/ppermute | solution.py:293
  50.3 10.7 %collective-permute-start.3 = (bf16[128,8,128]{2,1,0:T(8,128)(2,1)S(1)}, bf16[128,8,128]{2,1,0:T(8,128)(2,1)S(1)}, u32[]{:S(2)}, u32[]{:S(2)}) collective-permute-start(bf16[128,8,128]{2,1,0:T(8,128)(2,1)S(1)} %get-tuple-element.19.refs_2_), channel_id=1, source_target_pairs={{0,254},{2,0},{4,2},{6,4},{8,6},{10,8},{12,10},{14,12},{16,14},{18... | collective-permute-start | bytes 786440 | tf_op jit(solution)/shard_map/ppermute | solution.py:294
  50.4 23.4 %collective-permute-start.5 = (bf16[128,8,128]{2,1,0:T(8,128)(2,1)S(1)}, bf16[128,8,128]{2,1,0:T(8,128)(2,1)S(1)}, u32[]{:S(2)}, u32[]{:S(2)}) collective-permute-start(bf16[128,8,128]{2,1,0:T(8,128)(2,1)S(1)} %get-tuple-element.17.refs_0_.own_ref), channel_id=1, source_target_pairs={{0,1},{1,0},{2,3},{3,2},{4,5},{5,4},{6,7},{7,6},{8,9},{9,8},{10,11... | collective-permute-start | bytes 786440 | tf_op jit(solution)/shard_map/ppermute | solution.py:295
  61.6 13.3 %collective-permute-start.6 = (bf16[128,8,128]{2,1,0:T(8,128)(2,1)S(1)}, bf16[128,8,128]{2,1,0:T(8,128)(2,1)S(1)}, u32[]{:S(2)}, u32[]{:S(2)}) collective-permute-start(bf16[128,8,128]{2,1,0:T(8,128)(2,1)S(1)} %pick.2.refs_4_.right0_ref), channel_id=1, source_target_pairs={{0,1},{1,0},{2,3},{3,2},{4,5},{5,4},{6,7},{7,6},{8,9},{9,8},{10,11... | collective-permute-start | bytes 786440 | tf_op jit(solution)/shard_map/ppermute | solution.py:300
  62.3 18.5 %collective-permute-start.4 = (bf16[128,8,128]{2,1,0:T(8,128)(2,1)S(1)}, bf16[128,8,128]{2,1,0:T(8,128)(2,1)S(1)}, u32[]{:S(2)}, u32[]{:S(2)}) collective-permute-start(bf16[128,8,128]{2,1,0:T(8,128)(2,1)S(1)} %pick.3.right1_ref), channel_id=1, source_target_pairs={{0,1},{1,0},{2,3},{3,2},{4,5},{5,4},{6,7},{7,6},{8,9},{9,8},{10,11... | collective-permute-start | bytes 786440 | tf_op jit(solution)/shard_map/ppermute | solution.py:300

commit v3 on v2

--- a/solution.py
+++ b/solution.py
@@ -18,7 +18,7 @@
 TS = 1024
 RAW = 40
 ROWS = 8
-EDGE = 16
+EDGE = 4
 SHIFTS = 10
 PAIR = 2
 STEPS = MAXLAG // (SHIFTS * PAIR)
@@ -41,51 +41,47 @@
     return jnp.concatenate(parts, 0)
 
 
-def fold3(total):
-    return (total[:ROWS] + total[ROWS : 2 * ROWS]) + total[2 * ROWS :]
-
-
-def inner_kernel(band_ref, own_ref, out_ref):
-    band = split3(band_ref[:, EDGE : EDGE + RAW])
+def inner_kernel(band_ref, own_ref, inner_ref, to_left_ref, to_right_ref):
+    band = split3(band_ref[...])
+    count = band_ref.shape[0]
     for i in range(BLOCKS * CB // CHUNK):
         at = slice(i * CHUNK, (i + 1) * CHUNK)
-        out_ref[:, at] = fold3(jnp.dot(band, own_ref[:, at], preferred_element_type=F32))
+        total = jnp.dot(band, own_ref[:, at], preferred_element_type=F32)
+        total = (total[:count] + total[count : 2 * count]) + total[2 * count :]
+        inner_ref[:, at] = total[:ROWS]
+        to_left_ref[:, at] = total[ROWS : ROWS + EDGE]
+        to_right_ref[:, at] = total[ROWS + EDGE :]
 
 
 def inner_filter(band, own):
     return pl.pallas_call(
         inner_kernel,
         in_specs=[VMEM] * 2,
-        out_specs=VMEM,
-        out_shape=jax.ShapeDtypeStruct((ROWS, BLOCKS * CB), F32),
+        out_specs=[VMEM] * 3,
+        out_shape=[jax.ShapeDtypeStruct((n, BLOCKS * CB), F32) for n in (ROWS, EDGE, EDGE)],
         compiler_params=pltpu.CompilerParams(vmem_limit_bytes=24 << 20),
         name="inner_filter",
     )(band, own)
 
 
-def edge_kernel(band_ref, inner_ref, left_ref, right_ref, out_ref):
-    left_band = split3(band_ref[:, :EDGE])
-    right_band = split3(band_ref[:, EDGE + RAW :])
-    for i in range(BLOCKS * CB // CHUNK):
-        at = slice(i * CHUNK, (i + 1) * CHUNK)
-        edges = jnp.dot(left_band, left_ref[:, at], preferred_element_type=F32)
-        edges += jnp.dot(right_band, right_ref[:, at], preferred_element_type=F32)
-        rows = (inner_ref[:, at] + fold3(edges)).astype(BF16)
-        for j in range(CHUNK // CB):
-            for place, ahead in enumerate(DEALT):
-                owner = (i * (CHUNK // CB) + j - ahead) % BLOCKS
-                out_ref[owner, place] = rows[:, j * CB : (j + 1) * CB]
-
-
-def edge_filter(band, inner, left, right):
+def edge_kernel(inner_ref, left_ref, right_ref, out_ref):
+    for i in range(BLOCKS):
+        at = slice(i * CB, (i + 1) * CB)
+        edges = jnp.concatenate([left_ref[:, at], right_ref[:, at]], 0)
+        rows = (inner_ref[:, at] + edges).astype(BF16)
+        for place, ahead in enumerate(DEALT):
+            out_ref[(i - ahead) % BLOCKS, place] = rows
+
+
+def edge_filter(inner, left, right):
     return pl.pallas_call(
         edge_kernel,
-        in_specs=[VMEM] * 4,
+        in_specs=[VMEM] * 3,
         out_specs=VMEM,
         out_shape=jax.ShapeDtypeStruct((BLOCKS, len(DEALT), ROWS, CB), BF16),
         compiler_params=pltpu.CompilerParams(vmem_limit_bytes=24 << 20),
         name="edge_filter",
-    )(band, inner, left, right)
+    )(inner, left, right)
 
 
 BLOCK = jax.ShapeDtypeStruct((BLOCKS, ROWS, CB), BF16)
@@ -273,18 +269,27 @@
 
 
 def banded(filter_taps):
-    width = 2 * EDGE + RAW
-    rows = [jnp.pad(filter_taps, (1 + DECIM * m, width - 1 - DECIM * m - FILT)) for m in range(ROWS)]
+    blank = jnp.zeros((RAW,), filter_taps.dtype)
+
+    def row(m):
+        first = DECIM * m - FILT // 2
+        start = max(0, -first)
+        stop = min(FILT, RAW - first)
+        return jnp.pad(filter_taps[start:stop], (first + start, RAW - first - stop))
+
+    rows = [row(m) for m in range(ROWS)]
+    rows += [blank] + [row(m) for m in (-3, -2, -1)]
+    rows += [row(ROWS + m) for m in range(3)] + [blank]
     return jnp.stack(rows)
 
 
 def on_device(recording, filter_taps, pair_offsets):
     raw = recording[0]
     last = BLOCKS - 1
-    left = lax.ppermute(raw[RAW - EDGE :], "blk", [(i, i + 1) for i in range(last)])
-    right = lax.ppermute(raw[:EDGE], "blk", [(i + 1, i) for i in range(last)])
-    band = banded(filter_taps)
-    dealt = edge_filter(band, inner_filter(band, raw), left, right)
+    inner, to_left, to_right = inner_filter(banded(filter_taps), raw)
+    left = lax.ppermute(to_right, "blk", [(i, i + 1) for i in range(last)])
+    right = lax.ppermute(to_left, "blk", [(i + 1, i) for i in range(last)])
+    dealt = edge_filter(inner, left, right)
     arrived = lax.all_to_all(dealt, "blk", split_axis=0, concat_axis=0, tiled=True)
     seg = lax.axis_index("seg").astype(jnp.int32).reshape(1)
     odd = (lax.axis_index("blk") % 2).astype(jnp.int32).reshape(1)

time: 86.8 us -> 93.9 us (1.082)
  local copies, waits for them, and re-layouts: 2.43 us -> 10.7 us
  starting transfers between devices: 27.7 us -> 23.5 us
  waiting for transfers between devices: 30.6 us -> 33.9 us
    slice x1 -> x6, local copies, waits for them, and re-layouts: 1.37 us -> 4.86 us  [row(): return jnp.pad(filter_taps[start:stop], (first + start, RAW - first - stop))]
    ppermute x2, waiting for transfers between devices: 4.55 us -> 7.87 us  [the longest x1 6.51 us: on_device(): right = lax.ppermute(to_left, 'blk', [(i + 1, i) for i in range(last)])]
    another operation x2 -> x8, local copies, waits for them, and re-layouts: 1.05 us -> 3.89 us  [banded(): return jnp.stack(rows)]
    ppermute x2, starting transfers between devices: 7.67 us -> 4.98 us  [the longest x1 3.06 us: on_device(): left = lax.ppermute(to_right, 'blk', [(i, i + 1) for i in range(last)])]
    unnamed x4, local copies, waits for them, and re-layouts: 0.01 us -> 1.97 us
    all_to_all x1, starting transfers between devices: 15.8 us -> 14.6 us  [on_device(): lax.all_to_all(dealt, 'blk', split_axis=0, concat_axis=0, tiled=True)]
  transfers between devices with their start and end apart: 8 -> 8, of which waited for: 4 -> 4; matrix products, arithmetic and copies ran while one was open for 1% -> 0% of each run, Pallas kernels for 21% -> 19%
where the time goes in v3:
time: 93.9 us; the launch traced here: 93.5 us
  waiting for transfers between devices  33.9 us (36%)
  Pallas kernels  25.2 us (27%)
  starting transfers between devices  23.5 us (25%)
  local copies, waits for them, and re-layouts  10.7 us (11%)
    all_to_all x1, waiting for transfers between devices, on_device(): lax.all_to_all(dealt, 'blk', split_axis=0, concat_axis=0, tiled=True)  17.1 us
    all_to_all x1, starting transfers between devices, on_device(): lax.all_to_all(dealt, 'blk', split_axis=0, concat_axis=0, tiled=True)  14.6 us
    pallas_call x2, Pallas kernels, other_products(): pl.pallas_call(other_kernel, grid_spec=pltpu.PrefetchScalarGridSpec(num_s...  11.6 us
    ppermute x1, waiting for transfers between devices, on_device(): lax.ppermute(two, 'blk', [(i, (i - 1) % BLOCKS) for i in range(BLOCKS)])  8.92 us
    pallas_call x1, Pallas kernels, own_products(): pl.pallas_call(own_kernel, in_specs=[SMEM] + [VMEM] * 4, out_specs=[VMEM]...  8.43 us
    ppermute x1, waiting for transfers between devices, on_device(): right = lax.ppermute(to_left, 'blk', [(i + 1, i) for i in range(last)])  6.51 us
    slice x6, local copies, waits for them, and re-layouts, row(): return jnp.pad(filter_taps[start:stop], (first + start, RAW - first - stop))  4.86 us
    another operation x8, local copies, waits for them, and re-layouts, banded(): return jnp.stack(rows)  3.89 us
  transfers between devices with their start and end apart: 8, of which 4 were waited for; matrix products, arithmetic and copies ran while one was open for 0% of the time, Pallas kernels for 19%

profile of v3, /device:TPU:29, one launch (start us, length us, event | category | flops | bytes accessed | tf_op | source)
XLA Modules:
  0.0 93.5 jit_solution(5036190555715247007)
XLA Ops:
  0.0 1.2 %slice.42 = f32[1]{0:T(128)} slice(f32[31]{0:T(128)} %param.4), slice={[30:31]} | slice | bytes 8 | tf_op jit(solution)/shard_map/slice | solution.py:278
  1.2 0.7 slice.44
  2.0 0.7 slice.43
  2.7 0.7 slice.38
  3.4 0.7 slice.37
  4.9 0.8 pad_bitcast_fusion.9
  6.4 0.7 pad_bitcast_fusion.2
  7.1 0.8 pad_bitcast_fusion
  7.9 0.8 pad_bitcast_fusion.6
  8.8 1.3 %copy-done = bf16[1,40,16384]{2,1,0:T(8,128)(2,1)S(1)} copy-done((bf16[1,40,16384]{2,1,0:T(8,128)(2,1)S(1)}, bf16[1,40,16384]{2,1,0:T(8,128)(2,1)}, u32[]{:S(2)}) %copy-start) | copy-done | bytes 1310744
  10.8 3.1 %collective-permute-start = (f32[4,16384]{1,0:T(4,128)S(1)}, f32[4,16384]{1,0:T(4,128)S(1)}, u32[]{:S(2)}, u32[]{:S(2)}) collective-permute-start(f32[4,16384]{1,0:T(4,128)S(1)} %get-tuple-element.21), channel_id=1, source_target_pairs={{0,2},{2,4},{4,6},{6,8},{8,10},{10,12},{12,14},{14,16},{16,18},{18... | collective-permute-start | bytes 786440 | tf_op jit(solution)/shard_map/ppermute | solution.py:290
  13.8 1.9 %collective-permute-start.1 = (f32[4,16384]{1,0:T(4,128)S(1)}, f32[4,16384]{1,0:T(4,128)S(1)}, u32[]{:S(2)}, u32[]{:S(2)}) collective-permute-start(f32[4,16384]{1,0:T(4,128)S(1)} %get-tuple-element.22), channel_id=1, source_target_pairs={{2,0},{4,2},{6,4},{8,6},{10,8},{12,10},{14,12},{16,14},{18,16},{20... | collective-permute-start | bytes 786440 | tf_op jit(solution)/shard_map/ppermute | solution.py:291
  15.8 1.4 %collective-permute-done.left_ref = f32[4,16384]{1,0:T(4,128)S(1)} collective-permute-done((f32[4,16384]{1,0:T(4,128)S(1)}, f32[4,16384]{1,0:T(4,128)S(1)}, u32[]{:S(2)}, u32[]{:S(2)}) %collective-permute-start) | collective-permute-done | bytes 262176 | tf_op jit(solution)/shard_map/ppermute | solution.py:290
  17.1 6.5 %collective-permute-done.1.right_ref = f32[4,16384]{1,0:T(4,128)S(1)} collective-permute-done((f32[4,16384]{1,0:T(4,128)S(1)}, f32[4,16384]{1,0:T(4,128)S(1)}, u32[]{:S(2)}, u32[]{:S(2)}) %collective-permute-start.1) | collective-permute-done | bytes 262176 | tf_op jit(solution)/shard_map/ppermute | solution.py:291
  23.6 0.9 edge_filter.1
  24.6 14.6 %all-to-all-start = ((bf16[128,2,8,128]{3,2,1,0:T(8,128)(2,1)}), bf16[128,2,8,128]{3,2,1,0:T(8,128)(2,1)S(1)}, u32[]{:S(2)}, u32[]{:S(2)}) async-start(bf16[128,2,8,128]{3,2,1,0:T(8,128)(2,1)} %edge_filter.1), calls=%async_computation | async-start | bytes 1048576 | tf_op jit(solution)/shard_map/all_to_all | solution.py:293
  39.2 17.1 %all-to-all-done.arrived_ref = bf16[128,2,8,128]{3,2,1,0:T(8,128)(2,1)S(1)} async-done(((bf16[128,2,8,128]{3,2,1,0:T(8,128)(2,1)}), bf16[128,2,8,128]{3,2,1,0:T(8,128)(2,1)S(1)}, u32[]{:S(2)}, u32[]{:S(2)}) %all-to-all-start) | async-done | bytes 524320 | tf_op jit(solution)/shard_map/all_to_all | solution.py:293
  57.3 1.1 %left_rows.2 = (bf16[1280,1024]{1,0:T(8,128)(2,1)S(1)}, f32[128,128]{1,0:T(8,128)S(1)}) custom-call(s32[1]{0:T(128)} %bitcast.seg_ref, bf16[128,8,128]{2,1,0:T(8,128)(2,1)S(1)} %get-tuple-element.23.refs_0_.own_ref), custom_call_target="tpu_custom_call" | custom-call | flops 1048576 | bytes 9437184 | tf_op jit(solution)/shard_map/left_rows/pallas_call | solution.py:152
  58.4 8.9 %collective-permute-done.3.refs_3_ = bf16[128,8,128]{2,1,0:T(8,128)(2,1)S(1)} collective-permute-done((bf16[128,8,128]{2,1,0:T(8,128)(2,1)S(1)}, bf16[128,8,128]{2,1,0:T(8,128)(2,1)S(1)}, u32[]{:S(2)}, u32[]{:S(2)}) %collective-permute-start.3) | collective-permute-done | bytes 262176 | tf_op jit(solution)/shard_map/ppermute | solution.py:299
  69.3 3.0 %collective-permute-start.4 = (bf16[128,8,128]{2,1,0:T(8,128)(2,1)S(1)}, bf16[128,8,128]{2,1,0:T(8,128)(2,1)S(1)}, u32[]{:S(2)}, u32[]{:S(2)}) collective-permute-start(bf16[128,8,128]{2,1,0:T(8,128)(2,1)S(1)} %pick.3.right1_ref), channel_id=1, source_target_pairs={{0,1},{1,0},{2,3},{3,2},{4,5},{5,4},{6,7},{7,6},{8,9},{9,8},{10,11... | collective-permute-start | bytes 786440 | tf_op jit(solution)/shard_map/ppermute | solution.py:305
  72.3 8.4 %own_products.1 = (f32[10,1280,256]{2,1,0:T(8,128)S(1)}, f32[2,128,128]{2,1,0:T(8,128)S(1)}) custom-call(s32[1]{0:T(128)} %bitcast.seg_ref, bf16[1280,1024]{1,0:T(8,128)(2,1)S(1)} %get-tuple-element.26.lhs, f32[128,128]{1,0:T(8,128)S(1)} %get-tuple-element.27.column, bf16[128,8,128]{2,1,0:T(8,128)(2,1)S(1)} %pick.2.refs_4_.right0_ref, ...), custom_call_target="tpu_custom_call" | custom-call | flops 6710886400 | bytes 8388608 | tf_op jit(solution)/shard_map/own_products/pallas_call | solution.py:207
  80.8 1.2 %left_rows.3 = (bf16[1280,1024]{1,0:T(8,128)(2,1)S(1)}, f32[128,128]{1,0:T(8,128)S(1)}) custom-call(s32[1]{0:T(128)} %bitcast.seg_ref, bf16[128,8,128]{2,1,0:T(8,128)(2,1)S(1)} %collective-permute-done.5.own_ref), custom_call_target="tpu_custom_call" | custom-call | flops 1048576 | bytes 9437184 | tf_op jit(solution)/shard_map/left_rows/pallas_call | solution.py:152
  82.0 5.8 %other_products.2.refs_0_ = bf16[2,100,128,128]{3,2,1,0:T(8,128)(2,1)} custom-call(s32[1]{0:T(128)} %bitcast.seg_ref, bf16[128,8,128]{2,1,0:T(8,128)(2,1)S(1)} %collective-permute-done.6.other_ref, bf16[1280,1024]{1,0:T(8,128)(2,1)S(1)} %get-tuple-element.31.lhs, f32[128,128]{1,0:T(8,128)S(1)} %get-tuple-element.32.column, ...), custom_call_target="tpu_custom_call" | custom-call | flops 3355443200 | bytes 8388608 | tf_op jit(solution)/shard_map/other_products/pallas_call | solution.py:242
  87.8 5.8 %other_products.3 = bf16[2,100,128,128]{3,2,1,0:T(8,128)(2,1)} custom-call(s32[1]{0:T(128)} %bitcast.seg_ref, bf16[128,8,128]{2,1,0:T(8,128)(2,1)S(1)} %collective-permute-done.4.other_ref, bf16[1280,1024]{1,0:T(8,128)(2,1)S(1)} %get-tuple-element.31.lhs, f32[128,128]{1,0:T(8,128)S(1)} %get-tuple-element.32.column, ...), custom_call_target="tpu_custom_call", output_to_operand_aliasing={{}: (6, {})} | custom-call | flops 3355443200 | bytes 8388608 | tf_op jit(solution)/shard_map/other_products/pallas_call | solution.py:242
  (21 shorter events, 5.0 us)
Async XLA Ops:
  8.8 1.3 %copy-start = (bf16[1,40,16384]{2,1,0:T(8,128)(2,1)S(1)}, bf16[1,40,16384]{2,1,0:T(8,128)(2,1)}, u32[]{:S(2)}) copy-start(bf16[1,40,16384]{2,1,0:T(8,128)(2,1)} %param.3) | copy-start | bytes 3932164
  10.8 6.4 %collective-permute-start = (f32[4,16384]{1,0:T(4,128)S(1)}, f32[4,16384]{1,0:T(4,128)S(1)}, u32[]{:S(2)}, u32[]{:S(2)}) collective-permute-start(f32[4,16384]{1,0:T(4,128)S(1)} %get-tuple-element.21), channel_id=1, source_target_pairs={{0,2},{2,4},{4,6},{6,8},{8,10},{10,12},{12,14},{14,16},{16,18},{18... | collective-permute-start | bytes 786440 | tf_op jit(solution)/shard_map/ppermute | solution.py:290
  13.8 9.8 %collective-permute-start.1 = (f32[4,16384]{1,0:T(4,128)S(1)}, f32[4,16384]{1,0:T(4,128)S(1)}, u32[]{:S(2)}, u32[]{:S(2)}) collective-permute-start(f32[4,16384]{1,0:T(4,128)S(1)} %get-tuple-element.22), channel_id=1, source_target_pairs={{2,0},{4,2},{6,4},{8,6},{10,8},{12,10},{14,12},{16,14},{18,16},{20... | collective-permute-start | bytes 786440 | tf_op jit(solution)/shard_map/ppermute | solution.py:291
  24.6 31.7 %all-to-all-start = ((bf16[128,2,8,128]{3,2,1,0:T(8,128)(2,1)}), bf16[128,2,8,128]{3,2,1,0:T(8,128)(2,1)S(1)}, u32[]{:S(2)}, u32[]{:S(2)}) async-start(bf16[128,2,8,128]{3,2,1,0:T(8,128)(2,1)} %edge_filter.1), calls=%async_computation | async-start | bytes 1048576 | tf_op jit(solution)/shard_map/all_to_all | solution.py:293
  56.4 2.0 %collective-permute-start.2 = (bf16[128,8,128]{2,1,0:T(8,128)(2,1)S(1)}, bf16[128,8,128]{2,1,0:T(8,128)(2,1)S(1)}, u32[]{:S(2)}, u32[]{:S(2)}) collective-permute-start(bf16[128,8,128]{2,1,0:T(8,128)(2,1)S(1)} %get-tuple-element.24), channel_id=1, source_target_pairs={{0,2},{2,0},{4,6},{6,4},{8,10},{10,8},{12,14},{14,12},{16,18},{18,... | collective-permute-start | bytes 786440 | tf_op jit(solution)/shard_map/ppermute | solution.py:298
  56.9 10.4 %collective-permute-start.3 = (bf16[128,8,128]{2,1,0:T(8,128)(2,1)S(1)}, bf16[128,8,128]{2,1,0:T(8,128)(2,1)S(1)}, u32[]{:S(2)}, u32[]{:S(2)}) collective-permute-start(bf16[128,8,128]{2,1,0:T(8,128)(2,1)S(1)} %get-tuple-element.25.refs_2_), channel_id=1, source_target_pairs={{0,254},{2,0},{4,2},{6,4},{8,6},{10,8},{12,10},{14,12},{16,14},{18... | collective-permute-start | bytes 786440 | tf_op jit(solution)/shard_map/ppermute | solution.py:299
  57.0 23.7 %collective-permute-start.5 = (bf16[128,8,128]{2,1,0:T(8,128)(2,1)S(1)}, bf16[128,8,128]{2,1,0:T(8,128)(2,1)S(1)}, u32[]{:S(2)}, u32[]{:S(2)}) collective-permute-start(bf16[128,8,128]{2,1,0:T(8,128)(2,1)S(1)} %get-tuple-element.23.refs_0_.own_ref), channel_id=1, source_target_pairs={{0,1},{1,0},{2,3},{3,2},{4,5},{5,4},{6,7},{7,6},{8,9},{9,8},{10,11... | collective-permute-start | bytes 786440 | tf_op jit(solution)/shard_map/ppermute | solution.py:300
  67.4 0.7 copy-start.1
  68.6 13.4 %collective-permute-start.6 = (bf16[128,8,128]{2,1,0:T(8,128)(2,1)S(1)}, bf16[128,8,128]{2,1,0:T(8,128)(2,1)S(1)}, u32[]{:S(2)}, u32[]{:S(2)}) collective-permute-start(bf16[128,8,128]{2,1,0:T(8,128)(2,1)S(1)} %pick.2.refs_4_.right0_ref), channel_id=1, source_target_pairs={{0,1},{1,0},{2,3},{3,2},{4,5},{5,4},{6,7},{7,6},{8,9},{9,8},{10,11... | collective-permute-start | bytes 786440 | tf_op jit(solution)/shard_map/ppermute | solution.py:305
  69.3 18.5 %collective-permute-start.4 = (bf16[128,8,128]{2,1,0:T(8,128)(2,1)S(1)}, bf16[128,8,128]{2,1,0:T(8,128)(2,1)S(1)}, u32[]{:S(2)}, u32[]{:S(2)}) collective-permute-start(bf16[128,8,128]{2,1,0:T(8,128)(2,1)S(1)} %pick.3.right1_ref), channel_id=1, source_target_pairs={{0,1},{1,0},{2,3},{3,2},{4,5},{5,4},{6,7},{7,6},{8,9},{9,8},{10,11... | collective-permute-start | bytes 786440 | tf_op jit(solution)/shard_map/ppermute | solution.py:305
